TPU v7x, 32 devices: a whole 2x2x4 slice. The times are simulated.
32 devices in a mesh: grp: 2 (over x), ha: 16 (over z, y, core).
Axes of the slice: x: 2, y: 2, z: 4, core: 2. Of those that a mesh axis runs over, the one named last changes fastest.
Arguments:
- frames: bfloat16 [4, 16, 112, 384], P('grp', 'ha'), parts along dimension 0, may hold values from -6 to 6
- cache_first: bfloat16 [4, 16, 112, 384], P('grp', 'ha'), parts along dimension 0, may hold values from -5 to 5
- cache_second: bfloat16 [4, 16, 112, 384], P('grp', 'ha'), parts along dimension 0, may hold values from -5 to 5
- gain_first: float32 [384], replicated, may hold values from 0.1 to 1.9
- gain_second: float32 [384], replicated, may hold values from 0.1 to 1.9
- bias_first: float32 [384], replicated, may hold values from -3 to 3
- bias_second: float32 [384], replicated, may hold values from -3 to 3
- weight_first: bfloat16 [10368, 384], P(None, 'ha'), may hold values from -0.0625 to 0.0625
- weight_second: bfloat16 [10368, 384], P(None, 'ha'), may hold values from -0.0625 to 0.0625
- cotangent: bfloat16 [4, 16, 112, 384], P('grp', 'ha'), parts along dimension 0, may hold values from -6 to 6
Outputs:
- output: bfloat16 [4, 16, 112, 384], P('grp', 'ha'), parts along dimension 0
- grad_frames: bfloat16 [4, 16, 112, 384], P('grp', 'ha'), parts along dimension 0
There are 2 independent parts, one for each index of `grp`. A program takes and returns all parts, laid end to end along the dimension named above; an argument that names none is the same for every part. Nothing has to cross between parts.
All inputs are finite; a program needn't handle non-finite values.
Results may differ from a plain program's by a relative error of at most 0.006.
Values may be sent and summed in bfloat16 or wider, within the bound.
A program may use at most 128 MiB of HBM per device.

v0:
```python
import jax
import jax.numpy as jnp
from jax import lax
from jax.sharding import PartitionSpec as P


def extended_2(block, sides, width):
    for axis, dim in sides:
        count = lax.axis_size(axis)
        forward = [(i, i + 1) for i in range(count - 1)]
        backward = [(target, source) for source, target in forward]
        low = lax.ppermute(
            lax.slice_in_dim(block, block.shape[dim] - width, None, axis=dim), axis, forward
        )
        high = lax.ppermute(lax.slice_in_dim(block, 0, width, axis=dim), axis, backward)
        block = jnp.concatenate([low, block, high], axis=dim)
    return block


def normed_silu(values, scales):
    mean_square = jnp.mean(values * values, axis=-1, keepdims=True)
    inverse = lax.rsqrt(mean_square + 1e-06)
    normed = values * inverse * scales
    return normed * jax.nn.sigmoid(normed)


def silu_backward(values, scales, upstream):
    mean_square = jnp.mean(values * values, axis=-1, keepdims=True)
    inverse = lax.rsqrt(mean_square + 1e-06)
    normed = values * inverse * scales
    sigmoid_value = jax.nn.sigmoid(normed)
    scaled = scales * upstream * sigmoid_value * (1.0 + normed * (1.0 - sigmoid_value))
    return inverse * scaled - values * inverse**3 * jnp.mean(
        values * scaled, axis=-1, keepdims=True
    )


def tap_patches(padded, length, rows, columns, flipped):
    pieces = []
    for frame_tap in range(3):
        for row_tap in range(3):
            for col_tap in range(3):
                if flipped:
                    frame_start, row_start, col_start = (2 - frame_tap, 2 - row_tap, 2 - col_tap)
                else:
                    frame_start, row_start, col_start = (frame_tap, row_tap, col_tap)
                pieces.append(
                    padded[
                        frame_start : frame_start + length,
                        row_start : row_start + rows,
                        col_start : col_start + columns,
                    ]
                )
    return jnp.stack(pieces, axis=3)


def local(
    frames,
    cache_first,
    cache_second,
    gain_first,
    gain_second,
    bias_first,
    bias_second,
    weight_first,
    weight_second,
    cotangent,
):
    length, rows, columns, channels = frames.shape
    kernel_one, kernel_two = (
        lax.all_gather(weight_first, "ha", axis=1, tiled=True),
        lax.all_gather(weight_second, "ha", axis=1, tiled=True),
    )
    kernel_one = kernel_one.reshape(27, channels, channels)
    inputs = frames.astype(jnp.float32)
    first_act = normed_silu(inputs, gain_first).astype(jnp.bfloat16)
    extended = jnp.concatenate([cache_first, first_act], axis=0)
    padded = extended_2(extended, (("ha", 1),), 1)
    padded = jnp.pad(padded, ((0, 0), (0, 0), (1, 1), (0, 0)))
    patches = tap_patches(padded, length, rows, columns, False)
    middle = jnp.einsum("lrwtc,tco->lrwo", patches, kernel_one, preferred_element_type=jnp.float32)
    middle = (middle + bias_first).astype(jnp.bfloat16)
    middle_float = middle.astype(jnp.float32)
    kernel_two = kernel_two.reshape(27, channels, channels)
    second_act = normed_silu(middle_float, gain_second).astype(jnp.bfloat16)
    extended = jnp.concatenate([cache_second, second_act], axis=0)
    padded = extended_2(extended, (("ha", 1),), 1)
    padded = jnp.pad(padded, ((0, 0), (0, 0), (1, 1), (0, 0)))
    patches = tap_patches(padded, length, rows, columns, False)
    second_out = jnp.einsum(
        "lrwtc,tco->lrwo", patches, kernel_two, preferred_element_type=jnp.float32
    )
    output = (inputs + second_out + bias_second).astype(jnp.bfloat16)
    padded = extended_2(cotangent, (("ha", 1),), 1)
    padded = jnp.pad(padded, ((0, 2), (0, 0), (1, 1), (0, 0)))
    patches = tap_patches(padded, length, rows, columns, True)
    grad_second = jnp.einsum(
        "lrwto,tco->lrwc", patches, kernel_two, preferred_element_type=jnp.float32
    )
    grad_middle = silu_backward(middle_float, gain_second, grad_second).astype(jnp.bfloat16)
    padded = extended_2(grad_middle, (("ha", 1),), 1)
    padded = jnp.pad(padded, ((0, 2), (0, 0), (1, 1), (0, 0)))
    patches = tap_patches(padded, length, rows, columns, True)
    grad_first = jnp.einsum(
        "lrwto,tco->lrwc", patches, kernel_one, preferred_element_type=jnp.float32
    )
    grad_frames = (
        cotangent.astype(jnp.float32) + silu_backward(inputs, gain_first, grad_first)
    ).astype(jnp.bfloat16)
    return (output, grad_frames)


def solution(mesh):
    return jax.shard_map(
        local,
        mesh=mesh,
        in_specs=(
            P("grp", "ha", None, None),
            P("grp", "ha", None, None),
            P("grp", "ha", None, None),
            P(),
            P(),
            P(),
            P(),
            P(None, "ha"),
            P(None, "ha"),
            P("grp", "ha", None, None),
        ),
        out_specs=(P("grp", "ha", None, None), P("grp", "ha", None, None)),
        check_vma=False,
    )
```

profile of v0, /device:TPU:5, one launch (start us, length us, event | category | flops | bytes accessed | tf_op | source)
XLA Modules:
  0.0 223.4 jit_solution(1379792984267743407)
XLA Ops:
  8.0 0.7 all-gather.5.cloned.1.call-update
  8.7 1.0 fusion.91
  9.7 1.1 fusion.99
  10.8 1.0 pad_maximum_fusion
  11.8 2.6 %collective-permute-start.1 = (bf16[4,1,112,384]{3,2,0,1:T(8,128)(2,1)S(1)}, bf16[4,1,112,384]{3,2,0,1:T(8,128)(2,1)S(1)}, u32[]{:S(2)}, u32[]{:S(2)}) collective-permute-start(bf16[4,1,112,384]{3,2,0,1:T(8,128)(2,1)S(1)} %pad_maximum_fusion), channel_id=1, source_target_pairs={{1,0},{2,1},{3,2},{4,3},{5,4},{6,5},{7,6},{8,7},{9,8},{10,9},{11,1... | collective-permute-start | bytes 1032200 | tf_op jit(solution)/shard_map/ppermute | solution.py:15
  14.4 3.9 %collective-permute-start = (bf16[4,1,112,384]{3,2,0,1:T(8,128)(2,1)S(1)}, bf16[4,1,112,384]{3,2,0,1:T(8,128)(2,1)S(1)}, u32[]{:S(2)}, u32[]{:S(2)}) collective-permute-start(bf16[4,1,112,384]{3,2,0,1:T(8,128)(2,1)S(1)} %pad_maximum_fusion), channel_id=1, source_target_pairs={{0,1},{1,2},{2,3},{3,4},{4,5},{5,6},{6,7},{7,8},{8,9},{9,10},{10,1... | collective-permute-start | bytes 1032200 | tf_op jit(solution)/shard_map/ppermute | solution.py:12
  18.3 1.9 collective-permute-start.5
  20.2 4.5 %collective-permute-start.4 = (bf16[2,1,112,384]{3,2,0,1:T(8,128)(2,1)}, bf16[2,1,112,384]{3,2,0,1:T(8,128)(2,1)S(1)}, u32[]{:S(2)}, u32[]{:S(2)}) collective-permute-start(bf16[2,1,112,384]{3,2,0,1:T(8,128)(2,1)} %bitcast.545), channel_id=1, source_target_pairs={{0,1},{1,2},{2,3},{3,4},{4,5},{5,6},{6,7},{7,8},{8,9},{9,10},{10,1... | collective-permute-start | bytes 516104 | tf_op jit(solution)/shard_map/ppermute | solution.py:12
  24.8 0.7 constant_dynamic-update-slice_fusion.107
  27.7 0.7 constant_dynamic-update-slice_fusion.103
  29.8 0.7 constant_dynamic-update-slice_fusion.100
  30.5 0.9 collective-permute-done.5
  32.8 1.1 constant_dynamic-update-slice_fusion.26
  33.9 0.8 constant_dynamic-update-slice_fusion.25
  34.6 0.7 constant_dynamic-update-slice_fusion.24
  35.3 0.7 constant_dynamic-update-slice_fusion.23
  36.0 0.7 constant_dynamic-update-slice_fusion.22
  36.8 0.7 constant_dynamic-update-slice_fusion.21
  37.5 0.7 constant_dynamic-update-slice_fusion.20
  38.2 0.7 constant_dynamic-update-slice_fusion.19
  38.9 0.7 constant_dynamic-update-slice_fusion.18
  39.6 0.7 constant_dynamic-update-slice_fusion.17
  40.3 0.7 constant_dynamic-update-slice_fusion.16
  41.0 0.7 constant_dynamic-update-slice_fusion.15
  42.4 0.7 constant_dynamic-update-slice_fusion.13
  43.1 0.7 constant_dynamic-update-slice_fusion.12
  44.5 0.7 constant_dynamic-update-slice_fusion.10
  45.2 0.7 constant_dynamic-update-slice_fusion.9
  45.9 0.7 constant_dynamic-update-slice_fusion.8
  46.6 0.7 constant_dynamic-update-slice_fusion.7
  47.3 0.7 constant_dynamic-update-slice_fusion.6
  48.0 0.7 constant_dynamic-update-slice_fusion.5
  48.7 0.9 constant_dynamic-update-slice_fusion.4
  49.6 0.7 constant_dynamic-update-slice_fusion.3
  51.0 0.7 constant_dynamic-update-slice_fusion.1
  51.7 0.7 constant_dynamic-update-slice_fusion
  52.4 34.4 %all-gather.3.cloned.1.call-done = bf16[10368,384]{0,1:T(8,128)(2,1)} async-done(((bf16[10368,24]{0,1:T(8,128)(2,1)}), bf16[10368,384]{0,1:T(8,128)(2,1)}) %all-gather.3.cloned.1.call-update) | async-done | bytes 7962640 | tf_op jit(solution)/shard_map/all_gather | solution.py:71
  86.8 11.3 %copy.39 = bf16[10368,384]{1,0:T(8,128)(2,1)} copy(bf16[10368,384]{0,1:T(8,128)(2,1)} %all-gather.3.cloned.1.call-done) | data formatting | bytes 15925248 | tf_op jit(solution)/shard_map/all_gather | solution.py:71
  98.2 7.4 %multiply_reduce_fusion.1 = (f32[2,112]{1,0:T(2,128)S(1)}, f32[2,112,384]{2,1,0:T(8,128)S(1)}) fusion(f32[384]{0:T(512)S(1)} %copy-done.7, bf16[27,384,384,1]{2,1,0,3:T(8,128)(2,1)} %bitcast.528, bf16[2,1,112,27,384]{4,2,3,0,1:T(8,128)(2,1)} %constant_dynamic-update-slice_fusion), kind=kOutput, calls=%fused_computation.90 | convolution fusion | flops 1784057600 | bytes 12953984 | tf_op jit(solution)/shard_map/lrwtc,tco->lrwo/dot_general | solution.py:81
  105.6 54.0 %all-gather.5.cloned.1.call-done = bf16[10368,384]{0,1:T(8,128)(2,1)} async-done(((bf16[10368,24]{0,1:T(8,128)(2,1)}), bf16[10368,384]{0,1:T(8,128)(2,1)}) %all-gather.5.cloned.1.call-update) | async-done | bytes 7962640 | tf_op jit(solution)/shard_map/all_gather | solution.py:72
  159.6 11.3 %copy.41 = bf16[10368,384]{1,0:T(8,128)(2,1)} copy(bf16[10368,384]{0,1:T(8,128)(2,1)} %all-gather.5.cloned.1.call-done) | data formatting | bytes 15925248 | tf_op jit(solution)/shard_map/all_gather | solution.py:72
  170.9 7.7 %multiply_reduce_fusion = (f32[2,112]{1,0:T(2,128)S(1)}, f32[2,112,384]{2,1,0:T(8,128)S(1)}) fusion(f32[2,112,384]{2,1,0:T(8,128)S(1)} %get-tuple-element.11, f32[2,112]{1,0:T(2,128)S(1)} %get-tuple-element.9, bf16[27,384,384,1]{2,1,3,0:T(8,128)(2,1)} %bitcast.524, bf16[2,1,112,27,384]{4,2,0,3,1:T(8,128)(2,1)} %copy-done.5, f32[384]{0:T(512)S(1)} %copy-done.6), kind=kOutput, calls=%fused_computation.86 | convolution fusion | flops 1784745728 | bytes 13298944 | tf_op jit(solution)/shard_map/lrwto,tco->lrwc/dot_general | solution.py:97
  178.8 2.2 collective-permute-start.7
  181.0 4.3 %collective-permute-start.6 = (bf16[2,1,112,384]{3,2,0,1:T(8,128)(2,1)S(1)}, bf16[2,1,112,384]{3,2,0,1:T(8,128)(2,1)S(1)}, u32[]{:S(2)}, u32[]{:S(2)}) collective-permute-start(bf16[2,1,112,384]{3,2,0,1:T(8,128)(2,1)S(1)} %bitcast.542), channel_id=1, source_target_pairs={{0,1},{1,2},{2,3},{3,4},{4,5},{5,6},{6,7},{7,8},{8,9},{9,10},{10,1... | collective-permute-start | bytes 516104 | tf_op jit(solution)/shard_map/ppermute | solution.py:12
  185.3 0.7 constant_dynamic-update-slice_fusion.99
  186.1 1.9 collective-permute-start.3
  188.0 4.7 %collective-permute-start.2 = (bf16[4,1,112,384]{3,2,0,1:T(8,128)(2,1)S(1)}, bf16[4,1,112,384]{3,2,0,1:T(8,128)(2,1)S(1)}, u32[]{:S(2)}, u32[]{:S(2)}) collective-permute-start(bf16[4,1,112,384]{3,2,0,1:T(8,128)(2,1)S(1)} %pad_maximum_fusion.1), channel_id=1, source_target_pairs={{0,1},{1,2},{2,3},{3,4},{4,5},{5,6},{6,7},{7,8},{8,9},{9,10},{10,1... | collective-permute-start | bytes 1032200 | tf_op jit(solution)/shard_map/ppermute | solution.py:12
  192.9 0.7 constant_dynamic-update-slice_fusion.98
  193.6 0.7 constant_dynamic-update-slice_fusion.97
  195.0 0.7 constant_dynamic-update-slice_fusion.95
  195.7 0.7 constant_dynamic-update-slice_fusion.94
  196.4 0.7 constant_dynamic-update-slice_fusion.93
  197.1 0.7 constant_dynamic-update-slice_fusion.92
  197.9 0.7 constant_dynamic-update-slice_fusion.91
  198.6 0.7 constant_dynamic-update-slice_fusion.90
  199.3 0.7 constant_dynamic-update-slice_fusion.89
  200.0 0.7 constant_dynamic-update-slice_fusion.88
  201.3 0.7 constant_dynamic-update-slice_fusion.86
  202.7 0.7 constant_dynamic-update-slice_fusion.84
  203.4 0.7 constant_dynamic-update-slice_fusion.83
  204.1 0.7 constant_dynamic-update-slice_fusion.82
  205.5 5.4 %fusion.105 = (f32[2,112]{1,0:T(2,128)S(1)}, f32[2,1,112,384]{3,2,0,1:T(8,128)S(1)}) fusion(bf16[2,1,112,384]{3,2,1,0:T(8,128)(2,1)S(1)} %copy-done, f32[384]{0:T(512)S(1)} %copy-done.4, f32[2,112]{1,0:T(2,128)S(1)} %get-tuple-element.7, bf16[27,384,384,1]{2,1,3,0:T(8,128)(2,1)S(1)} %bitcast.531, ...), kind=kOutput, calls=%fused_computation.84 | convolution fusion | flops 1784831744 | bytes 13126912 | tf_op jit(solution)/shard_map/lrwto,tco->lrwc/dot_general | solution.py:104
  210.9 0.8 fusion.106
  213.3 3.3 %fusion.68 = bf16[2,1,112,384]{3,2,1,0:T(8,128)(2,1)} fusion(bf16[27,384,384,1]{2,1,3,0:T(8,128)(2,1)S(1)} %bitcast.527, bf16[2,1,112,27,384]{4,2,0,3,1:T(8,128)(2,1)S(1)} %constant_dynamic-update-slice_fusion.27, bf16[2,1,112,384]{3,2,1,0:T(8,128)(2,1)S(1)} %copy-done, f32[384]{0:T(512)S(1)} %copy-done.8), kind=kOutput, calls=%fused_computation.37 | convolution fusion | flops 1783971840 | bytes 12953088 | tf_op jit(solution)/shard_map/lrwtc,tco->lrwo/dot_general | solution.py:90
  (114 shorter events, 12.3 us)
Async XLA Ops:
  7.2 24.2 %copy-start.3 = (bf16[2,1,112,384]{3,2,1,0:T(8,128)(2,1)S(1)}, bf16[2,1,112,384]{3,2,1,0:T(8,128)(2,1)}, u32[]{:S(2)}) copy-start(bf16[2,1,112,384]{3,2,1,0:T(8,128)(2,1)} %param.19) | copy-start | bytes 516100
  7.2 79.7 %all-gather.3.cloned.1.call-start = ((), (), s32[]{:S(2)}) async-start(), calls=%async_computation | async-start | bytes 8460288 | tf_op jit(solution)/shard_map/all_gather | solution.py:71
  7.9 151.6 %all-gather.5.cloned.1.call-start = ((), (), s32[]{:S(2)}) async-start(), calls=%async_computation.1 | async-start | bytes 8460288 | tf_op jit(solution)/shard_map/all_gather | solution.py:72
  11.8 20.7 %collective-permute-start.1 = (bf16[4,1,112,384]{3,2,0,1:T(8,128)(2,1)S(1)}, bf16[4,1,112,384]{3,2,0,1:T(8,128)(2,1)S(1)}, u32[]{:S(2)}, u32[]{:S(2)}) collective-permute-start(bf16[4,1,112,384]{3,2,0,1:T(8,128)(2,1)S(1)} %pad_maximum_fusion), channel_id=1, source_target_pairs={{1,0},{2,1},{3,2},{4,3},{5,4},{6,5},{7,6},{8,7},{9,8},{10,9},{11,1... | collective-permute-start | bytes 1032200 | tf_op jit(solution)/shard_map/ppermute | solution.py:15
  14.4 18.1 %collective-permute-start = (bf16[4,1,112,384]{3,2,0,1:T(8,128)(2,1)S(1)}, bf16[4,1,112,384]{3,2,0,1:T(8,128)(2,1)S(1)}, u32[]{:S(2)}, u32[]{:S(2)}) collective-permute-start(bf16[4,1,112,384]{3,2,0,1:T(8,128)(2,1)S(1)} %pad_maximum_fusion), channel_id=1, source_target_pairs={{0,1},{1,2},{2,3},{3,4},{4,5},{5,6},{6,7},{7,8},{8,9},{9,10},{10,1... | collective-permute-start | bytes 1032200 | tf_op jit(solution)/shard_map/ppermute | solution.py:12
  18.3 13.1 %collective-permute-start.5 = (bf16[2,1,112,384]{3,2,0,1:T(8,128)(2,1)}, bf16[2,1,112,384]{3,2,0,1:T(8,128)(2,1)S(1)}, u32[]{:S(2)}, u32[]{:S(2)}) collective-permute-start(bf16[2,1,112,384]{3,2,0,1:T(8,128)(2,1)} %bitcast.544), channel_id=1, source_target_pairs={{1,0},{2,1},{3,2},{4,3},{5,4},{6,5},{7,6},{8,7},{9,8},{10,9},{11,1... | collective-permute-start | bytes 516104 | tf_op jit(solution)/shard_map/ppermute | solution.py:15
  20.2 11.2 %collective-permute-start.4 = (bf16[2,1,112,384]{3,2,0,1:T(8,128)(2,1)}, bf16[2,1,112,384]{3,2,0,1:T(8,128)(2,1)S(1)}, u32[]{:S(2)}, u32[]{:S(2)}) collective-permute-start(bf16[2,1,112,384]{3,2,0,1:T(8,128)(2,1)} %bitcast.545), channel_id=1, source_target_pairs={{0,1},{1,2},{2,3},{3,4},{4,5},{5,6},{6,7},{7,8},{8,9},{9,10},{10,1... | collective-permute-start | bytes 516104 | tf_op jit(solution)/shard_map/ppermute | solution.py:12
  25.6 6.8 %copy-start.1 = (bf16[2,1,112,384]{3,2,1,0:T(8,128)(2,1)S(1)}, bf16[2,1,112,384]{3,2,1,0:T(8,128)(2,1)}, u32[]{:S(2)}) copy-start(bf16[2,1,112,384]{3,2,1,0:T(8,128)(2,1)} %param.11) | copy-start | bytes 516100
  32.4 15.6 %copy-start.5 = (bf16[2,1,112,27,384]{4,2,0,3,1:T(8,128)(2,1)}, bf16[2,1,112,27,384]{4,2,0,3,1:T(8,128)(2,1)S(1)}, u32[]{:S(2)}) copy-start(bf16[2,1,112,27,384]{4,2,0,3,1:T(8,128)(2,1)S(1)} %constant_dynamic-update-slice_fusion.54) | copy-start | bytes 13934596
  32.4 16.3 %copy-start = (bf16[2,1,112,384]{3,2,1,0:T(8,128)(2,1)S(1)}, bf16[2,1,112,384]{3,2,1,0:T(8,128)(2,1)}, u32[]{:S(2)}) copy-start(bf16[2,1,112,384]{3,2,1,0:T(8,128)(2,1)} %param.10) | copy-start | bytes 516100
  32.4 16.3 %copy-start.4 = (f32[384]{0:T(512)S(1)}, f32[384]{0:T(512)}, u32[]{:S(2)}) copy-start(f32[384]{0:T(512)} %param.13) | copy-start | bytes 4612
  52.4 45.8 %copy-start.7 = (f32[384]{0:T(512)S(1)}, f32[384]{0:T(512)}, u32[]{:S(2)}) copy-start(f32[384]{0:T(512)} %param.15) | copy-start | bytes 4612
  105.6 65.3 %copy-start.6 = (f32[384]{0:T(512)S(1)}, f32[384]{0:T(512)}, u32[]{:S(2)}) copy-start(f32[384]{0:T(512)} %param.14) | copy-start | bytes 4612
  170.8 34.7 %slice-start.2 = ((s8[7962624]{0:T(1024)(128)(4,1)}), s8[4194304]{0:T(1024)(128)(4,1)S(1)}, s32[]{:S(2)}) async-start(s8[7962624]{0:T(1024)(128)(4,1)} %bitcast.529), calls=%async_computation.4 | async-start | bytes 8388608
  170.9 15.2 %copy-start.2 = (bf16[2,1,112,384]{3,2,1,0:T(8,128)(2,1)S(1)}, bf16[2,1,112,384]{3,2,1,0:T(8,128)(2,1)}, u32[]{:S(2)}) copy-start(bf16[2,1,112,384]{3,2,1,0:T(8,128)(2,1)} %param.12) | copy-start | bytes 516100
  170.9 34.6 %slice-start.3 = ((s8[7962624]{0:T(1024)(128)(4,1)}), s8[3768320]{0:T(1024)(128)(4,1)S(1)}, s32[]{:S(2)}) async-start(s8[7962624]{0:T(1024)(128)(4,1)} %bitcast.529), calls=%async_computation.5 | async-start | bytes 7536640
  178.8 13.9 %collective-permute-start.7 = (bf16[2,1,112,384]{3,2,0,1:T(8,128)(2,1)S(1)}, bf16[2,1,112,384]{3,2,0,1:T(8,128)(2,1)S(1)}, u32[]{:S(2)}, u32[]{:S(2)}) collective-permute-start(bf16[2,1,112,384]{3,2,0,1:T(8,128)(2,1)S(1)} %bitcast.541), channel_id=1, source_target_pairs={{1,0},{2,1},{3,2},{4,3},{5,4},{6,5},{7,6},{8,7},{9,8},{10,9},{11,1... | collective-permute-start | bytes 516104 | tf_op jit(solution)/shard_map/ppermute | solution.py:15
  181.0 11.7 %collective-permute-start.6 = (bf16[2,1,112,384]{3,2,0,1:T(8,128)(2,1)S(1)}, bf16[2,1,112,384]{3,2,0,1:T(8,128)(2,1)S(1)}, u32[]{:S(2)}, u32[]{:S(2)}) collective-permute-start(bf16[2,1,112,384]{3,2,0,1:T(8,128)(2,1)S(1)} %bitcast.542), channel_id=1, source_target_pairs={{0,1},{1,2},{2,3},{3,4},{4,5},{5,6},{6,7},{7,8},{8,9},{9,10},{10,1... | collective-permute-start | bytes 516104 | tf_op jit(solution)/shard_map/ppermute | solution.py:12
  186.1 25.7 %collective-permute-start.3 = (bf16[4,1,112,384]{3,2,0,1:T(8,128)(2,1)S(1)}, bf16[4,1,112,384]{3,2,0,1:T(8,128)(2,1)S(1)}, u32[]{:S(2)}, u32[]{:S(2)}) collective-permute-start(bf16[4,1,112,384]{3,2,0,1:T(8,128)(2,1)S(1)} %pad_maximum_fusion.1), channel_id=1, source_target_pairs={{1,0},{2,1},{3,2},{4,3},{5,4},{6,5},{7,6},{8,7},{9,8},{10,9},{11,1... | collective-permute-start | bytes 1032200 | tf_op jit(solution)/shard_map/ppermute | solution.py:15
  188.0 23.8 %collective-permute-start.2 = (bf16[4,1,112,384]{3,2,0,1:T(8,128)(2,1)S(1)}, bf16[4,1,112,384]{3,2,0,1:T(8,128)(2,1)S(1)}, u32[]{:S(2)}, u32[]{:S(2)}) collective-permute-start(bf16[4,1,112,384]{3,2,0,1:T(8,128)(2,1)S(1)} %pad_maximum_fusion.1), channel_id=1, source_target_pairs={{0,1},{1,2},{2,3},{3,4},{4,5},{5,6},{6,7},{7,8},{8,9},{9,10},{10,1... | collective-permute-start | bytes 1032200 | tf_op jit(solution)/shard_map/ppermute | solution.py:12
  205.5 7.8 %slice-start = ((s8[7962624]{0:T(1024)(128)(4,1)}), s8[4194304]{0:T(1024)(128)(4,1)S(1)}, s32[]{:S(2)}) async-start(s8[7962624]{0:T(1024)(128)(4,1)} %bitcast.525), calls=%async_computation.2 | async-start | bytes 8388608
  205.5 7.8 %slice-start.1 = ((s8[7962624]{0:T(1024)(128)(4,1)}), s8[3768320]{0:T(1024)(128)(4,1)S(1)}, s32[]{:S(2)}) async-start(s8[7962624]{0:T(1024)(128)(4,1)} %bitcast.525), calls=%async_computation.3 | async-start | bytes 7536640
  212.1 1.2 copy-start.8
Sparse Core Ops, SparseCore 0:
  10.2 76.6 all-gather.2
  89.0 70.5 all-gather.4
where the time goes:
time: 224 us; the launch traced here: 223 us
  waiting for transfers between devices  90.7 us (40%)
  local copies, waits for them, and re-layouts  61.4 us (27%)
  starting transfers between devices  26.1 us (12%)
  matrix products  23.8 us (11%)
  between operations  14.6 us (7%)
  other arithmetic  6.78 us (3%)
    all_gather x1, waiting for transfers between devices, local(): lax.all_gather(weight_second, 'ha', axis=1, tiled=True)  54 us
    unnamed x127, local copies, waits for them, and re-layouts  37.3 us
    all_gather x1, waiting for transfers between devices, local(): lax.all_gather(weight_first, 'ha', axis=1, tiled=True)  34.4 us
    ppermute x4, starting transfers between devices, extended_2(): lax.ppermute(lax.slice_in_dim(block, block.shape[dim] - width, None, axis...  17.4 us
    all_gather x1, local copies, waits for them, and re-layouts, local(): lax.all_gather(weight_first, 'ha', axis=1, tiled=True)  11.3 us
    all_gather x1, local copies, waits for them, and re-layouts, local(): lax.all_gather(weight_second, 'ha', axis=1, tiled=True)  11.3 us
    ppermute x4, starting transfers between devices, extended_2(): lax.ppermute(lax.slice_in_dim(block, 0, width, axis=dim), axis, backward)  8.59 us
    dot_general x1, matrix products, local(): jnp.einsum('lrwto,tco->lrwc', patches, kernel_two, preferred_element_type...  7.75 us
  transfers between devices with their start and end apart: 10, of which 3 were waited for; matrix products, arithmetic and copies ran while one was open for 30% of the time, Pallas kernels for 0%

commit v1 on v0

--- a/solution.py
+++ b/solution.py
@@ -1,6 +1,10 @@
+import functools
+
 import jax
 import jax.numpy as jnp
 from jax import lax
+from jax.experimental import pallas as pl
+from jax.experimental.pallas import tpu as pltpu
 from jax.sharding import PartitionSpec as P
 
 
@@ -54,7 +58,7 @@
     return jnp.stack(pieces, axis=3)
 
 
-def local(
+def local_general(
     frames,
     cache_first,
     cache_second,
@@ -110,9 +114,436 @@
     return (output, grad_frames)
 
 
+MESH = pl.DeviceIdType.MESH
+LINE_AHEAD = 3
+
+
+def block_kernel(
+    n,
+    groups,
+    columns,
+    frames_ref,
+    cache_first_ref,
+    cache_second_ref,
+    gain_first_ref,
+    gain_second_ref,
+    bias_first_ref,
+    bias_second_ref,
+    cotangent_ref,
+    shards,
+    output_ref,
+    grad_ref,
+    buf,
+    weights,
+    early,
+    act,
+    grad_mid,
+    patches_one,
+    patches_two,
+    acc,
+    acc_t,
+    middle_ref,
+    z_send,
+    z_recv,
+    y_send,
+    y_recv,
+    x_send,
+    x_recv,
+    s_send,
+    s_recv,
+    t_send,
+    t_recv,
+    halo_send,
+    halo_recv,
+    local_sem,
+):
+    f32, bf16 = jnp.float32, jnp.bfloat16
+    chunks, width, lanes = shards.shape
+    half = chunks // 2
+    channels = lanes // 3
+    two = 2 * columns
+    length = n // 4
+    me = lax.axis_index("ha")
+    group = lax.axis_index("grp")
+    core = lax.rem(me, 2)
+    row = lax.rem(me // 2, 2)
+    line = me // 4
+    odd = lax.rem(group, 2)
+    own_off = pl.multiple_of(odd * channels, 128)
+    give_off = pl.multiple_of(odd * 2 * channels, 128)
+    take_off = pl.multiple_of((1 - odd) * 2 * channels, 128)
+
+    def at(line_, row_, core_):
+        return {"ha": (line_ * 2 + row_) * 2 + core_}
+
+    sibling = at(line, row, 1 - core)
+    across = at(line, 1 - row, core)
+    twin = {"grp": group + 1 - 2 * odd}
+
+    def line_peer(step):
+        return at(lax.rem(line + step, length), row, core)
+
+    barrier = pltpu.get_barrier_semaphore()
+    partners = [sibling, across, twin] + [line_peer(s) for s in range(1, length)]
+    for partner in partners:
+        pl.semaphore_signal(barrier, inc=1, device_id=partner, device_id_type=MESH)
+
+    has_low, has_high = me > 0, me < n - 1
+
+    @pl.when(has_low)
+    def _():
+        pl.semaphore_signal(barrier, inc=1, device_id={"ha": me - 1}, device_id_type=MESH)
+
+    @pl.when(has_high)
+    def _():
+        pl.semaphore_signal(barrier, inc=1, device_id={"ha": me + 1}, device_id_type=MESH)
+
+    keep = pltpu.make_async_copy(
+        shards.at[:, :, pl.ds(own_off, 2 * channels)],
+        buf.at[:, core, row, line, :, pl.ds(own_off, 2 * channels)],
+        local_sem,
+    )
+    keep.start()
+    pl.semaphore_wait(
+        barrier, len(partners) + has_low.astype(jnp.int32) + has_high.astype(jnp.int32)
+    )
+
+    def remote(src, dst, send, recv, device):
+        return pltpu.make_async_remote_copy(
+            src_ref=src, dst_ref=dst, send_sem=send, recv_sem=recv, device_id=device, device_id_type=MESH
+        )
+
+    def z_copy(q, step, source):
+        return remote(
+            shards.at[q, :, pl.ds(own_off, 2 * channels)],
+            buf.at[q, core, row, source, :, pl.ds(own_off, 2 * channels)],
+            z_send.at[q, step - 1],
+            z_recv.at[q, step - 1],
+            line_peer(step),
+        )
+
+    def same(view, send, recv, device):
+        return remote(view, view, send, recv, device)
+
+    def y_copy(q, row_):
+        view = buf.at[q, core, row_, :, :, pl.ds(own_off, 2 * channels)]
+        return same(view, y_send.at[q], y_recv.at[q], across)
+
+    def x_copy(q, offset):
+        view = buf.at[q, core, :, :, :, pl.ds(offset, channels)]
+        return same(view, x_send.at[q], x_recv.at[q], twin)
+
+    def s_copy(q, core_):
+        view = buf.at[q, core_, :, :, :, pl.ds(own_off, 2 * channels)]
+        return same(view, s_send.at[q], s_recv.at[q], sibling)
+
+    def t_copy(q, core_):
+        view = buf.at[q, core_, :, :, :, pl.ds(take_off, channels)]
+        return same(view, t_send.at[q], t_recv.at[q], sibling)
+
+    def z_start(q):
+        for step in range(1, length):
+            z_copy(q, step, line).start()
+
+    def halo_copies(ref, index):
+        low = remote(
+            ref.at[1], ref.at[2], halo_send.at[index, 0], halo_recv.at[index, 0], {"ha": me - 1}
+        )
+        high = remote(
+            ref.at[1], ref.at[0], halo_send.at[index, 1], halo_recv.at[index, 1], {"ha": me + 1}
+        )
+        return low, high
+
+    def halo_start(ref, index):
+        low, high = halo_copies(ref, index)
+
+        @pl.when(has_low)
+        def _():
+            low.start()
+
+        @pl.when(has_high)
+        def _():
+            high.start()
+
+    def halo_wait(ref, index):
+        low, high = halo_copies(ref, index)
+
+        @pl.when(has_low)
+        def _():
+            high.wait_recv()
+            low.wait_send()
+
+        @pl.when(has_high)
+        def _():
+            low.wait_recv()
+            high.wait_send()
+
+        @pl.when(jnp.logical_not(has_low))
+        def _():
+            ref[0] = jnp.zeros(ref.shape[1:], ref.dtype)
+
+        @pl.when(jnp.logical_not(has_high))
+        def _():
+            ref[2] = jnp.zeros(ref.shape[1:], ref.dtype)
+
+    def comm(t):
+        q = t + LINE_AHEAD + 4
+
+        @pl.when(q < chunks)
+        def _():
+            z_start(q)
+
+        q_z = t + 3
+
+        @pl.when(q_z < chunks)
+        def _():
+            for step in range(1, length):
+                z_copy(q_z, step, lax.rem(line - step + length, length)).wait_recv()
+            y_copy(q_z, row).start()
+
+        q_y = t + 2
+
+        @pl.when(jnp.logical_and(q_y >= 0, q_y < chunks))
+        def _():
+            y_copy(q_y, 1 - row).wait_recv()
+            x_copy(q_y, give_off).start()
+            s_copy(q_y, core).start()
+
+        q_x = t + 1
+
+        @pl.when(jnp.logical_and(q_x >= 0, q_x < chunks))
+        def _():
+            x_copy(q_x, take_off).wait_recv()
+            t_copy(q_x, core).start()
+
+        @pl.when(t >= 0)
+        def _():
+            s_copy(t, 1 - core).wait_recv()
+            t_copy(t, 1 - core).wait_recv()
+            for index in range(n):
+                weights[t, index * width : (index + 1) * width, :] = buf[
+                    t, index % 2, index // 2 % 2, index // 4
+                ]
+
+    def column(shape):
+        return lax.rem(lax.broadcasted_iota(jnp.int32, shape, 0), columns)
+
+    def shifted(value, by):
+        rolled = pltpu.roll(value, by % value.shape[0], 0)
+        edge = 0 if by > 0 else columns - 1
+        return jnp.where(column(value.shape) == edge, 0.0, rolled)
+
+    def unfold(src, src_start, dst, dst_start, count):
+        for j in range(3):
+            value = src[j, src_start : src_start + count, :]
+            wide = value.astype(f32)
+            rows = slice(dst_start, dst_start + count)
+            dst[j, rows, :channels] = shifted(wide, 1).astype(bf16)
+            dst[j, rows, channels : 2 * channels] = value
+            dst[j, rows, 2 * channels :] = shifted(wide, -1).astype(bf16)
+
+    def forward_dot(patches, q, i, j):
+        left = patches[j, pl.ds(pl.multiple_of(i * columns, 16), two), :]
+        acc[...] += lax.dot_general(
+            left, weights[q], (((1,), (1,)), ((), ())), preferred_element_type=f32
+        )
+
+    def back_late(ref, start, q, j):
+        acc_t[...] += jnp.dot(
+            ref[2 - j, start : start + two, :], weights[q], preferred_element_type=f32
+        )
+
+    def back_early(ref, start, q, j):
+        acc_t[:columns, :] += jnp.dot(
+            ref[2 - j, start + columns : start + two, :], weights[q], preferred_element_type=f32
+        )
+
+    def folded():
+        return (
+            shifted(acc_t[:, :channels], -1)
+            + acc_t[:, channels : 2 * channels]
+            + shifted(acc_t[:, 2 * channels :], 1)
+        )
+
+    for q in range(min(LINE_AHEAD + 1, chunks)):
+        z_start(q)
+
+    early[1, :two, :] = cache_first_ref[...]
+    early[1, two : 2 * two, :] = normed_silu(frames_ref[...].astype(f32), gain_first_ref[...]).astype(bf16)
+    early[1, 2 * two : 3 * two, :] = cache_second_ref[...]
+    early[1, 3 * two :, :] = cotangent_ref[...]
+    halo_start(early, 0)
+    keep.wait()
+
+    @pl.loop(-LINE_AHEAD, 0)
+    def _(t):
+        comm(t)
+
+    halo_wait(early, 0)
+    unfold(early, 0, patches_one, 0, 2 * two)
+    unfold(early, 2 * two, patches_two, 0, two)
+    acc[...] = jnp.zeros(acc.shape, f32)
+
+    @pl.loop(0, half)
+    def _(t):
+        comm(t)
+        forward_dot(patches_one, t, t // 3, lax.rem(t, 3))
+
+    middle_ref[...] = (acc[...] + bias_first_ref[...]).astype(bf16)
+    act[1] = normed_silu(middle_ref[...].astype(f32), gain_second_ref[...]).astype(bf16)
+    halo_start(act, 1)
+    acc[...] = jnp.zeros(acc.shape, f32)
+    acc_t[...] = jnp.zeros(acc_t.shape, f32)
+    comm(half)
+    halo_wait(act, 1)
+    unfold(act, 0, patches_two, two, two)
+
+    @pl.loop(0, 3)
+    def _(j):
+        @pl.when(j > 0)
+        def _():
+            comm(half + j)
+
+        back_late(early, 3 * two, half + j, j)
+        forward_dot(patches_two, half + j, 2, j)
+
+    @pl.loop(0, 3)
+    def _(j):
+        comm(half + 3 + j)
+        back_early(early, 3 * two, half + 3 + j, j)
+        forward_dot(patches_two, half + 3 + j, 1, j)
+
+    grad_mid[1] = silu_backward(
+        middle_ref[...].astype(f32), gain_second_ref[...], folded()
+    ).astype(bf16)
+    halo_start(grad_mid, 2)
+    acc_t[...] = jnp.zeros(acc_t.shape, f32)
+    comm(half + 6)
+    forward_dot(patches_two, half + 6, 0, 0)
+    halo_wait(grad_mid, 2)
+
+    @pl.loop(0, 3)
+    def _(j):
+        back_late(grad_mid, 0, 6 + j, j)
+        back_early(grad_mid, 0, 3 + j, j)
+
+        @pl.when(j > 0)
+        def _():
+            comm(half + 6 + j)
+            forward_dot(patches_two, half + 6 + j, 0, j)
+
+    inputs = frames_ref[...].astype(f32)
+    output_ref[...] = (inputs + acc[...] + bias_second_ref[...]).astype(bf16)
+    grad_ref[...] = (
+        cotangent_ref[...].astype(f32) + silu_backward(inputs, gain_first_ref[...], folded())
+    ).astype(bf16)
+
+    @pl.loop(0, chunks)
+    def _(q):
+        for step in range(1, length):
+            z_copy(q, step, line).wait_send()
+        y_copy(q, row).wait_send()
+        x_copy(q, give_off).wait_send()
+        s_copy(q, core).wait_send()
+        t_copy(q, core).wait_send()
+
+
+def local_fused(
+    n,
+    groups,
+    frames,
+    cache_first,
+    cache_second,
+    gain_first,
+    gain_second,
+    bias_first,
+    bias_second,
+    weight_first,
+    weight_second,
+    cotangent,
+):
+    _, _, columns, channels = frames.shape
+    rows, width = weight_first.shape
+    f32, bf16 = jnp.float32, jnp.bfloat16
+    lanes = 3 * channels
+    two = 2 * columns
+    one = weight_first.T.reshape(width, 9, lanes).transpose(1, 0, 2)
+    other = weight_second.T.reshape(width, 9, lanes).transpose(1, 0, 2)
+    shards = jnp.concatenate([one, other[6:], other[3:6], other[:3]], axis=0)
+    flat = lambda value: value.reshape(two, channels)
+    vector = lambda value: value.reshape(1, channels)
+    vmem = pl.BlockSpec(memory_space=pltpu.VMEM)
+    dma = pltpu.SemaphoreType.DMA
+    chunks, length = 18, n // 4
+    outputs = pl.pallas_call(
+        functools.partial(block_kernel, n, groups, columns),
+        out_shape=[jax.ShapeDtypeStruct((two, channels), bf16)] * 2,
+        in_specs=[vmem] * 9,
+        out_specs=[vmem] * 2,
+        scratch_shapes=[
+            pltpu.VMEM((chunks, 2, 2, length, width, lanes), bf16),
+            pltpu.VMEM((chunks, channels, lanes), bf16),
+            pltpu.VMEM((3, 4 * two, channels), bf16),
+            pltpu.VMEM((3, two, channels), bf16),
+            pltpu.VMEM((3, two, channels), bf16),
+            pltpu.VMEM((3, 2 * two, lanes), bf16),
+            pltpu.VMEM((3, 2 * two, lanes), bf16),
+            pltpu.VMEM((two, channels), f32),
+            pltpu.VMEM((two, lanes), f32),
+            pltpu.VMEM((two, channels), bf16),
+            dma((chunks, length - 1)),
+            dma((chunks, length - 1)),
+            dma((chunks,)),
+            dma((chunks,)),
+            dma((chunks,)),
+            dma((chunks,)),
+            dma((chunks,)),
+            dma((chunks,)),
+            dma((chunks,)),
+            dma((chunks,)),
+            dma((3, 2)),
+            dma((3, 2)),
+            dma,
+        ],
+        compiler_params=pltpu.CompilerParams(
+            collective_id=0, has_side_effects=True, vmem_limit_bytes=60 * 1024 * 1024
+        ),
+        cost_estimate=pl.CostEstimate(
+            flops=6 * two * rows * channels, bytes_accessed=8 * rows * width, transcendentals=0
+        ),
+    )(
+        flat(frames),
+        flat(cache_first),
+        flat(cache_second),
+        vector(gain_first),
+        vector(gain_second),
+        vector(bias_first),
+        vector(bias_second),
+        flat(cotangent),
+        shards,
+    )
+    return tuple(value.reshape(frames.shape) for value in outputs)
+
+
+def local(n, groups, *arrays):
+    frames, weight = arrays[0], arrays[7]
+    fits = (
+        n % 4 == 0
+        and n >= 8
+        and groups % 2 == 0
+        and frames.shape[:2] == (2, 1)
+        and frames.shape[2] % 16 == 0
+        and frames.shape[3] % 128 == 0
+        and weight.shape[1] % 8 == 0
+    )
+    if fits:
+        return local_fused(n, groups, *arrays)
+    return local_general(*arrays)
+
+
 def solution(mesh):
     return jax.shard_map(
-        local,
+        functools.partial(local, mesh.shape["ha"], mesh.shape["grp"]),
         mesh=mesh,
         in_specs=(
             P("grp", "ha", None, None),

time: 224 us -> 117 us (0.52)
  the two profiles are of different devices: /device:TPU:5 before, /device:TPU:17 now
where the time goes in v1:
time: 117 us
  Pallas kernels  108 us (92%)
  local copies, waits for them, and re-layouts  7.07 us (6%)
    pallas_call x1, Pallas kernels, local_fused(): pl.pallas_call(functools.partial(block_kernel, n, groups, columns), out_s...  108 us
    unnamed x14, local copies, waits for them, and re-layouts  3.65 us

profile of v1, /device:TPU:17, one launch (start us, length us, event | category | flops | bytes accessed | tf_op | source)
XLA Modules:
  0.0 116.6 jit_solution(14601624404409230628)
XLA Ops:
  0.6 1.1 copy.22
  1.7 0.0 copy-start
  1.8 1.0 copy-done
  2.8 0.0 copy-start.2
  2.8 1.1 pad_maximum_fusion.shards
  3.9 0.0 copy-done.2
  3.9 0.0 copy-start.3
  3.9 0.6 reshape.43.gain_first_ref
  4.5 0.1 copy-done.3
  4.6 0.0 copy-start.4
  4.6 0.6 reshape.44.gain_second_ref
  5.2 0.1 copy-done.4
  5.3 0.0 copy-start.5
  5.3 0.6 reshape.45.bias_first_ref
  5.9 0.1 copy-done.5
  6.0 0.6 reshape.46.bias_second_ref
  6.5 107.7 %shard_map.113 = (bf16[224,384]{1,0:T(8,128)(2,1)}, bf16[224,384]{1,0:T(8,128)(2,1)}) custom-call(bf16[224,384]{1,0:T(8,128)(2,1)} %bitcast.32, bf16[224,384]{1,0:T(8,128)(2,1)} %bitcast.33, bf16[224,384]{1,0:T(8,128)(2,1)} %bitcast.34, f32[1,384]{1,0:T(1,128)} %reshape.43.gain_first_ref, f32[1,384]{1,0:T(1,128)} %reshape.44.gain_second_ref, ...), custom_call_target="tpu_custom_call" | custom-call | flops 5350883328 | bytes 1990656 | tf_op jit(solution)/shard_map/pallas_call | solution.py:478
  114.3 0.0 copy-start.1
  114.3 1.6 %copy.26 = bf16[2,1,112,384]{3,2,1,0:T(8,128)(2,1)} copy(bf16[2,1,112,384]{3,2,1,0:T(8,128)(2,1)} %bitcast.31) | data formatting | bytes 344064
  115.9 0.0 copy-done.1
  116.0 0.7 copy.27
  (2 shorter events, 0.1 us)
Async XLA Ops:
  1.7 1.0 copy-start
  2.8 1.1 copy-start.2
  3.9 0.7 copy-start.3
  4.6 0.7 copy-start.4
  5.3 0.7 copy-start.5
  114.3 1.7 %copy-start.1 = (bf16[224,384]{1,0:T(8,128)(2,1)S(1)}, bf16[224,384]{1,0:T(8,128)(2,1)}, u32[]{:S(2)}) copy-start(bf16[224,384]{1,0:T(8,128)(2,1)} %get-tuple-element.5) | copy-start | bytes 516100

commit v2 on v1

--- a/solution.py
+++ b/solution.py
@@ -115,7 +115,8 @@
 
 
 MESH = pl.DeviceIdType.MESH
-LINE_AHEAD = 3
+DEPTH = 2
+LINE_AHEAD = 3 * DEPTH
 
 
 def block_kernel(
@@ -293,7 +294,7 @@
         def _():
             z_start(q)
 
-        q_z = t + 3
+        q_z = t + LINE_AHEAD
 
         @pl.when(q_z < chunks)
         def _():
@@ -301,7 +302,7 @@
                 z_copy(q_z, step, lax.rem(line - step + length, length)).wait_recv()
             y_copy(q_z, row).start()
 
-        q_y = t + 2
+        q_y = t + 2 * DEPTH
 
         @pl.when(jnp.logical_and(q_y >= 0, q_y < chunks))
         def _():
@@ -309,7 +310,7 @@
             x_copy(q_y, give_off).start()
             s_copy(q_y, core).start()
 
-        q_x = t + 1
+        q_x = t + DEPTH
 
         @pl.when(jnp.logical_and(q_x >= 0, q_x < chunks))
         def _():
@@ -365,11 +366,11 @@
             + shifted(acc_t[:, 2 * channels :], 1)
         )
 
-    for q in range(min(LINE_AHEAD + 1, chunks)):
+    for q in range(min(4, chunks)):
         z_start(q)
 
     early[1, :two, :] = cache_first_ref[...]
-    early[1, two : 2 * two, :] = normed_silu(frames_ref[...].astype(f32), gain_first_ref[...]).astype(bf16)
+    early[1, two : 2 * two, :] = normed_silu(frames_ref[...].astype(f32), gain_first_ref[...].reshape(1, channels)).astype(bf16)
     early[1, 2 * two : 3 * two, :] = cache_second_ref[...]
     early[1, 3 * two :, :] = cotangent_ref[...]
     halo_start(early, 0)
@@ -389,37 +390,38 @@
         comm(t)
         forward_dot(patches_one, t, t // 3, lax.rem(t, 3))
 
-    middle_ref[...] = (acc[...] + bias_first_ref[...]).astype(bf16)
-    act[1] = normed_silu(middle_ref[...].astype(f32), gain_second_ref[...]).astype(bf16)
+    middle_ref[...] = (acc[...] + bias_first_ref[...].reshape(1, channels)).astype(bf16)
+    act[1] = normed_silu(middle_ref[...].astype(f32), gain_second_ref[...].reshape(1, channels)).astype(bf16)
     halo_start(act, 1)
     acc[...] = jnp.zeros(acc.shape, f32)
     acc_t[...] = jnp.zeros(acc_t.shape, f32)
-    comm(half)
+
+    @pl.loop(0, 3)
+    def _(j):
+        comm(half + j)
+        back_late(early, 3 * two, half + j, j)
+
     halo_wait(act, 1)
     unfold(act, 0, patches_two, two, two)
-
-    @pl.loop(0, 3)
-    def _(j):
-        @pl.when(j > 0)
-        def _():
-            comm(half + j)
-
-        back_late(early, 3 * two, half + j, j)
-        forward_dot(patches_two, half + j, 2, j)
 
     @pl.loop(0, 3)
     def _(j):
         comm(half + 3 + j)
         back_early(early, 3 * two, half + 3 + j, j)
+        forward_dot(patches_two, half + j, 2, j)
         forward_dot(patches_two, half + 3 + j, 1, j)
 
     grad_mid[1] = silu_backward(
-        middle_ref[...].astype(f32), gain_second_ref[...], folded()
+        middle_ref[...].astype(f32), gain_second_ref[...].reshape(1, channels), folded()
     ).astype(bf16)
     halo_start(grad_mid, 2)
     acc_t[...] = jnp.zeros(acc_t.shape, f32)
-    comm(half + 6)
-    forward_dot(patches_two, half + 6, 0, 0)
+
+    @pl.loop(0, 2)
+    def _(j):
+        comm(half + 6 + j)
+        forward_dot(patches_two, half + 6 + j, 0, j)
+
     halo_wait(grad_mid, 2)
 
     @pl.loop(0, 3)
@@ -427,15 +429,13 @@
         back_late(grad_mid, 0, 6 + j, j)
         back_early(grad_mid, 0, 3 + j, j)
 
-        @pl.when(j > 0)
-        def _():
-            comm(half + 6 + j)
-            forward_dot(patches_two, half + 6 + j, 0, j)
+    comm(half + 8)
+    forward_dot(patches_two, half + 8, 0, 2)
 
     inputs = frames_ref[...].astype(f32)
-    output_ref[...] = (inputs + acc[...] + bias_second_ref[...]).astype(bf16)
+    output_ref[...] = (inputs + acc[...] + bias_second_ref[...].reshape(1, channels)).astype(bf16)
     grad_ref[...] = (
-        cotangent_ref[...].astype(f32) + silu_backward(inputs, gain_first_ref[...], folded())
+        cotangent_ref[...].astype(f32) + silu_backward(inputs, gain_first_ref[...].reshape(1, channels), folded())
     ).astype(bf16)
 
     @pl.loop(0, chunks)
@@ -471,7 +471,6 @@
     other = weight_second.T.reshape(width, 9, lanes).transpose(1, 0, 2)
     shards = jnp.concatenate([one, other[6:], other[3:6], other[:3]], axis=0)
     flat = lambda value: value.reshape(two, channels)
-    vector = lambda value: value.reshape(1, channels)
     vmem = pl.BlockSpec(memory_space=pltpu.VMEM)
     dma = pltpu.SemaphoreType.DMA
     chunks, length = 18, n // 4
@@ -515,10 +514,10 @@
         flat(frames),
         flat(cache_first),
         flat(cache_second),
-        vector(gain_first),
-        vector(gain_second),
-        vector(bias_first),
-        vector(bias_second),
+        gain_first,
+        gain_second,
+        bias_first,
+        bias_second,
         flat(cotangent),
         shards,
     )

time: 117 us -> 113 us (0.966)
  the two profiles are of different devices: /device:TPU:17 before, /device:TPU:1 now
where the time goes in v2:
time: 113 us
  Pallas kernels  107 us (95%)
  local copies, waits for them, and re-layouts  3.57 us (3%)
  other arithmetic  1.14 us (1%)
    pallas_call x1, Pallas kernels, local_fused(): pl.pallas_call(functools.partial(block_kernel, n, groups, columns), out_s...  107 us
    unnamed x6, local copies, waits for them, and re-layouts  2.36 us

profile of v2, /device:TPU:1, one launch (start us, length us, event | category | flops | bytes accessed | tf_op | source)
XLA Modules:
  0.0 112.7 jit_solution(14918646584469811531)
XLA Ops:
  0.6 0.0 copy-start
  0.6 1.1 %copy.23 = bf16[3,9,8,1152]{3,2,0,1:T(8,128)(2,1)S(1)} copy(bf16[3,9,8,1152]{3,2,1,0:T(8,128)(2,1)} %bitcast.28) | data formatting | bytes 995328 | tf_op jit(solution)/shard_map/reshape | solution.py:470
  1.8 0.0 copy-done
  1.9 1.1 %pad_maximum_fusion.shards = bf16[18,24,1152]{2,1,0:T(8,128)(2,1)} fusion(bf16[3,24,1152]{2,1,0:T(8,128)(2,1)S(1)} %get-tuple-element.11, bf16[3,24,1152]{2,1,0:T(8,128)(2,1)S(1)} %get-tuple-element.12, bf16[3,24,1152]{2,1,0:T(8,128)(2,1)S(1)} %get-tuple-element.10, bf16[9,24,1152]{2,1,0:T(8,128)(2,1)S(1)} %bitcast.27), kind=kLoop, calls=%fused_computation | loop fusion | flops 1492992 | bytes 1990656 | tf_op jit(solution)/shard_map/concatenate | solution.py:472
  3.0 107.3 %shard_map.113 = (bf16[224,384]{1,0:T(8,128)(2,1)}, bf16[224,384]{1,0:T(8,128)(2,1)}) custom-call(bf16[224,384]{1,0:T(8,128)(2,1)} %bitcast.32, bf16[224,384]{1,0:T(8,128)(2,1)} %bitcast.33, bf16[224,384]{1,0:T(8,128)(2,1)} %bitcast.34, f32[384]{0:T(512)} %gain_first_ref.1, f32[384]{0:T(512)} %gain_second_ref.1, f32[384]{0:T(512)} %bias_first_ref.1, ...), custom_call_target="tpu_custom_call" | custom-call | flops 5350883328 | bytes 1990656 | tf_op jit(solution)/shard_map/pallas_call | solution.py:477
  110.3 0.0 copy-start.1
  110.4 1.6 %copy.26 = bf16[2,1,112,384]{3,2,1,0:T(8,128)(2,1)} copy(bf16[2,1,112,384]{3,2,1,0:T(8,128)(2,1)} %bitcast.31) | data formatting | bytes 344064
  112.0 0.0 copy-done.1
  112.0 0.7 copy.27
  (2 shorter events, 0.1 us)
Async XLA Ops:
  0.6 1.2 %copy-start = (bf16[10368,24]{0,1:T(8,128)(2,1)S(1)}, bf16[10368,24]{0,1:T(8,128)(2,1)}, u32[]{:S(2)}) copy-start(bf16[10368,24]{0,1:T(8,128)(2,1)} %param.18) | copy-start | bytes 1492996
  110.3 1.7 %copy-start.1 = (bf16[224,384]{1,0:T(8,128)(2,1)S(1)}, bf16[224,384]{1,0:T(8,128)(2,1)}, u32[]{:S(2)}) copy-start(bf16[224,384]{1,0:T(8,128)(2,1)} %get-tuple-element.5) | copy-start | bytes 516100

commit v3 on v2

--- a/solution.py
+++ b/solution.py
@@ -159,9 +159,12 @@
     local_sem,
 ):
     f32, bf16 = jnp.float32, jnp.bfloat16
-    chunks, width, lanes = shards.shape
+    chunks, tiles, width, _ = shards.shape
     half = chunks // 2
+    lanes = tiles * 128
     channels = lanes // 3
+    give = tiles // 2
+    own = tiles - give
     two = 2 * columns
     length = n // 4
     me = lax.axis_index("ha")
@@ -170,9 +173,9 @@
     row = lax.rem(me // 2, 2)
     line = me // 4
     odd = lax.rem(group, 2)
-    own_off = pl.multiple_of(odd * channels, 128)
-    give_off = pl.multiple_of(odd * 2 * channels, 128)
-    take_off = pl.multiple_of((1 - odd) * 2 * channels, 128)
+    own_part = pl.ds(odd * give, own)
+    give_part = pl.ds(odd * own, give)
+    take_part = pl.ds((1 - odd) * own, give)
 
     def at(line_, row_, core_):
         return {"ha": (line_ * 2 + row_) * 2 + core_}
@@ -200,8 +203,8 @@
         pl.semaphore_signal(barrier, inc=1, device_id={"ha": me + 1}, device_id_type=MESH)
 
     keep = pltpu.make_async_copy(
-        shards.at[:, :, pl.ds(own_off, 2 * channels)],
-        buf.at[:, core, row, line, :, pl.ds(own_off, 2 * channels)],
+        shards,
+        buf.at[:, core, row, line],
         local_sem,
     )
     keep.start()
@@ -216,8 +219,8 @@
 
     def z_copy(q, step, source):
         return remote(
-            shards.at[q, :, pl.ds(own_off, 2 * channels)],
-            buf.at[q, core, row, source, :, pl.ds(own_off, 2 * channels)],
+            shards.at[q, own_part],
+            buf.at[q, core, row, source, own_part],
             z_send.at[q, step - 1],
             z_recv.at[q, step - 1],
             line_peer(step),
@@ -227,19 +230,24 @@
         return remote(view, view, send, recv, device)
 
     def y_copy(q, row_):
-        view = buf.at[q, core, row_, :, :, pl.ds(own_off, 2 * channels)]
+        view = buf.at[q, core, row_, :, own_part]
         return same(view, y_send.at[q], y_recv.at[q], across)
 
-    def x_copy(q, offset):
-        view = buf.at[q, core, :, :, :, pl.ds(offset, channels)]
-        return same(view, x_send.at[q], x_recv.at[q], twin)
+    def x_one(q, step, part):
+        source = lax.rem(line - step + length, length)
+        view = buf.at[q, core, row, source, part]
+        return same(view, x_send.at[q, step - 1], x_recv.at[q, step - 1], twin)
+
+    def x_rest(q, part):
+        view = buf.at[q, core, 1 - row, :, part]
+        return same(view, x_send.at[q, length - 1], x_recv.at[q, length - 1], twin)
 
     def s_copy(q, core_):
-        view = buf.at[q, core_, :, :, :, pl.ds(own_off, 2 * channels)]
+        view = buf.at[q, core_, :, :, own_part]
         return same(view, s_send.at[q], s_recv.at[q], sibling)
 
     def t_copy(q, core_):
-        view = buf.at[q, core_, :, :, :, pl.ds(take_off, channels)]
+        view = buf.at[q, core_, :, :, take_part]
         return same(view, t_send.at[q], t_recv.at[q], sibling)
 
     def z_start(q):
@@ -301,20 +309,24 @@
             for step in range(1, length):
                 z_copy(q_z, step, lax.rem(line - step + length, length)).wait_recv()
             y_copy(q_z, row).start()
+            for step in range(1, length):
+                x_one(q_z, step, give_part).start()
 
         q_y = t + 2 * DEPTH
 
         @pl.when(jnp.logical_and(q_y >= 0, q_y < chunks))
         def _():
             y_copy(q_y, 1 - row).wait_recv()
-            x_copy(q_y, give_off).start()
+            x_rest(q_y, give_part).start()
             s_copy(q_y, core).start()
 
         q_x = t + DEPTH
 
         @pl.when(jnp.logical_and(q_x >= 0, q_x < chunks))
         def _():
-            x_copy(q_x, take_off).wait_recv()
+            for step in range(1, length):
+                x_one(q_x, step, take_part).wait_recv()
+            x_rest(q_x, take_part).wait_recv()
             t_copy(q_x, core).start()
 
         @pl.when(t >= 0)
@@ -322,9 +334,11 @@
             s_copy(t, 1 - core).wait_recv()
             t_copy(t, 1 - core).wait_recv()
             for index in range(n):
-                weights[t, index * width : (index + 1) * width, :] = buf[
-                    t, index % 2, index // 2 % 2, index // 4
-                ]
+                rows = slice(index * width, (index + 1) * width)
+                for m in range(tiles):
+                    weights[t, rows, m * 128 : (m + 1) * 128] = buf[
+                        t, index % 2, index // 2 % 2, index // 4, m
+                    ]
 
     def column(shape):
         return lax.rem(lax.broadcasted_iota(jnp.int32, shape, 0), columns)
@@ -442,8 +456,9 @@
     def _(q):
         for step in range(1, length):
             z_copy(q, step, line).wait_send()
+            x_one(q, step, give_part).wait_send()
         y_copy(q, row).wait_send()
-        x_copy(q, give_off).wait_send()
+        x_rest(q, give_part).wait_send()
         s_copy(q, core).wait_send()
         t_copy(q, core).wait_send()
 
@@ -467,8 +482,9 @@
     f32, bf16 = jnp.float32, jnp.bfloat16
     lanes = 3 * channels
     two = 2 * columns
-    one = weight_first.T.reshape(width, 9, lanes).transpose(1, 0, 2)
-    other = weight_second.T.reshape(width, 9, lanes).transpose(1, 0, 2)
+    tiles = lanes // 128
+    one = weight_first.T.reshape(width, 9, tiles, 128).transpose(1, 2, 0, 3)
+    other = weight_second.T.reshape(width, 9, tiles, 128).transpose(1, 2, 0, 3)
     shards = jnp.concatenate([one, other[6:], other[3:6], other[:3]], axis=0)
     flat = lambda value: value.reshape(two, channels)
     vmem = pl.BlockSpec(memory_space=pltpu.VMEM)
@@ -480,7 +496,7 @@
         in_specs=[vmem] * 9,
         out_specs=[vmem] * 2,
         scratch_shapes=[
-            pltpu.VMEM((chunks, 2, 2, length, width, lanes), bf16),
+            pltpu.VMEM((chunks, 2, 2, length, tiles, width, 128), bf16),
             pltpu.VMEM((chunks, channels, lanes), bf16),
             pltpu.VMEM((3, 4 * two, channels), bf16),
             pltpu.VMEM((3, two, channels), bf16),
@@ -494,8 +510,8 @@
             dma((chunks, length - 1)),
             dma((chunks,)),
             dma((chunks,)),
-            dma((chunks,)),
-            dma((chunks,)),
+            dma((chunks, length)),
+            dma((chunks, length)),
             dma((chunks,)),
             dma((chunks,)),
             dma((chunks,)),

time: 113 us -> 110 us (0.973)
  the two profiles are of different devices: /device:TPU:1 before, /device:TPU:5 now
where the time goes in v3:
time: 110 us
  Pallas kernels  103 us (94%)
  local copies, waits for them, and re-layouts  5.11 us (5%)
  other arithmetic  1.11 us (1%)
    pallas_call x1, Pallas kernels, local_fused(): pl.pallas_call(functools.partial(block_kernel, n, groups, columns), out_s...  103 us
    unnamed x6, local copies, waits for them, and re-layouts  3.2 us

profile of v3, /device:TPU:5, one launch (start us, length us, event | category | flops | bytes accessed | tf_op | source)
XLA Modules:
  0.0 109.9 jit_solution(13157409391574167002)
XLA Ops:
  0.6 1.3 %reshape.32 = bf16[24,9,9,128]{3,2,1,0:T(8,128)(2,1)S(1)} reshape(bf16[24,10368]{1,0:T(8,128)(2,1)} %bitcast.20) | data formatting | bytes 995328 | tf_op jit(solution)/shard_map/reshape | solution.py:486
  1.9 0.0 copy-start
  2.0 0.1 copy.21
  2.1 0.9 copy-done
  3.0 0.3 reshape.33
  3.3 0.1 copy.20
  3.4 0.1 fusion
  3.5 1.1 %pad_maximum_fusion.shards = bf16[18,9,24,128]{3,2,1,0:T(8,128)(2,1)} fusion(bf16[3,9,24,128]{3,2,1,0:T(8,128)(2,1)S(1)} %get-tuple-element.11, bf16[3,9,24,128]{3,2,1,0:T(8,128)(2,1)S(1)} %get-tuple-element.12, bf16[3,9,24,128]{3,2,1,0:T(8,128)(2,1)S(1)} %get-tuple-element.10, bf16[9,9,24,128]{3,2,1,0:T(8,128)(2,1)S(1)} %bitcast.19), kind=kLoop, calls=%fused_computation | loop fusion | flops 1492992 | bytes 1990656 | tf_op jit(solution)/shard_map/concatenate | solution.py:488
  4.6 103.0 %shard_map.113 = (bf16[224,384]{1,0:T(8,128)(2,1)}, bf16[224,384]{1,0:T(8,128)(2,1)}) custom-call(bf16[224,384]{1,0:T(8,128)(2,1)} %bitcast.24, bf16[224,384]{1,0:T(8,128)(2,1)} %bitcast.25, bf16[224,384]{1,0:T(8,128)(2,1)} %bitcast.26, f32[384]{0:T(512)} %gain_first_ref.1, f32[384]{0:T(512)} %gain_second_ref.1, f32[384]{0:T(512)} %bias_first_ref.1, ...), custom_call_target="tpu_custom_call" | custom-call | flops 5350883328 | bytes 1990656 | tf_op jit(solution)/shard_map/pallas_call | solution.py:493
  107.6 0.0 copy-start.1
  107.6 1.6 %copy.24 = bf16[2,1,112,384]{3,2,1,0:T(8,128)(2,1)} copy(bf16[2,1,112,384]{3,2,1,0:T(8,128)(2,1)} %bitcast.23) | data formatting | bytes 344064
  109.3 0.0 copy-done.1
  109.3 0.7 copy.25
Async XLA Ops:
  1.9 1.0 copy-start
  107.6 1.7 %copy-start.1 = (bf16[224,384]{1,0:T(8,128)(2,1)S(1)}, bf16[224,384]{1,0:T(8,128)(2,1)}, u32[]{:S(2)}) copy-start(bf16[224,384]{1,0:T(8,128)(2,1)} %get-tuple-element.5) | copy-start | bytes 516100

commit v4 on v3

--- a/solution.py
+++ b/solution.py
@@ -358,9 +358,9 @@
             dst[j, rows, 2 * channels :] = shifted(wide, -1).astype(bf16)
 
     def forward_dot(patches, q, i, j):
-        left = patches[j, pl.ds(pl.multiple_of(i * columns, 16), two), :]
+        window = patches[j, pl.ds(pl.multiple_of(i * columns, 16), two), :]
         acc[...] += lax.dot_general(
-            left, weights[q], (((1,), (1,)), ((), ())), preferred_element_type=f32
+            weights[q], window, (((1,), (1,)), ((), ())), preferred_element_type=f32
         )
 
     def back_late(ref, start, q, j):
@@ -390,13 +390,18 @@
     halo_start(early, 0)
     keep.wait()
 
-    @pl.loop(-LINE_AHEAD, 0)
+    @pl.loop(-LINE_AHEAD, -DEPTH)
     def _(t):
         comm(t)
 
     halo_wait(early, 0)
     unfold(early, 0, patches_one, 0, 2 * two)
     unfold(early, 2 * two, patches_two, 0, two)
+
+    @pl.loop(-DEPTH, 0)
+    def _(t):
+        comm(t)
+
     acc[...] = jnp.zeros(acc.shape, f32)
 
     @pl.loop(0, half)
@@ -404,7 +409,7 @@
         comm(t)
         forward_dot(patches_one, t, t // 3, lax.rem(t, 3))
 
-    middle_ref[...] = (acc[...] + bias_first_ref[...].reshape(1, channels)).astype(bf16)
+    middle_ref[...] = (acc[...].T + bias_first_ref[...].reshape(1, channels)).astype(bf16)
     act[1] = normed_silu(middle_ref[...].astype(f32), gain_second_ref[...].reshape(1, channels)).astype(bf16)
     halo_start(act, 1)
     acc[...] = jnp.zeros(acc.shape, f32)
@@ -447,7 +452,7 @@
     forward_dot(patches_two, half + 8, 0, 2)
 
     inputs = frames_ref[...].astype(f32)
-    output_ref[...] = (inputs + acc[...] + bias_second_ref[...].reshape(1, channels)).astype(bf16)
+    output_ref[...] = (inputs + acc[...].T + bias_second_ref[...].reshape(1, channels)).astype(bf16)
     grad_ref[...] = (
         cotangent_ref[...].astype(f32) + silu_backward(inputs, gain_first_ref[...].reshape(1, channels), folded())
     ).astype(bf16)
@@ -503,7 +508,7 @@
             pltpu.VMEM((3, two, channels), bf16),
             pltpu.VMEM((3, 2 * two, lanes), bf16),
             pltpu.VMEM((3, 2 * two, lanes), bf16),
-            pltpu.VMEM((two, channels), f32),
+            pltpu.VMEM((channels, two), f32),
             pltpu.VMEM((two, lanes), f32),
             pltpu.VMEM((two, channels), bf16),
             dma((chunks, length - 1)),

time: 110 us -> 113 us (1.027); the launches traced: 110 us -> 111 us
  no operation moved by 1% of the time
where the time goes in v4:
time: 113 us; the launch traced here: 111 us
  Pallas kernels  104 us (92%)
  local copies, waits for them, and re-layouts  5.11 us (5%)
    pallas_call x1, Pallas kernels, local_fused(): pl.pallas_call(functools.partial(block_kernel, n, groups, columns), out_s...  104 us
    unnamed x6, local copies, waits for them, and re-layouts  3.2 us

profile of v4, /device:TPU:5, one launch (start us, length us, event | category | flops | bytes accessed | tf_op | source)
XLA Modules:
  0.0 111.0 jit_solution(3330875519245119087)
XLA Ops:
  0.6 1.3 %reshape.32 = bf16[24,9,9,128]{3,2,1,0:T(8,128)(2,1)S(1)} reshape(bf16[24,10368]{1,0:T(8,128)(2,1)} %bitcast.20) | data formatting | bytes 995328 | tf_op jit(solution)/shard_map/reshape | solution.py:491
  1.9 0.0 copy-start
  2.0 0.1 copy.21
  2.1 0.9 copy-done
  3.0 0.3 reshape.33
  3.3 0.1 copy.20
  3.4 0.1 fusion
  3.5 1.1 %pad_maximum_fusion.shards = bf16[18,9,24,128]{3,2,1,0:T(8,128)(2,1)} fusion(bf16[3,9,24,128]{3,2,1,0:T(8,128)(2,1)S(1)} %get-tuple-element.11, bf16[3,9,24,128]{3,2,1,0:T(8,128)(2,1)S(1)} %get-tuple-element.12, bf16[3,9,24,128]{3,2,1,0:T(8,128)(2,1)S(1)} %get-tuple-element.10, bf16[9,9,24,128]{3,2,1,0:T(8,128)(2,1)S(1)} %bitcast.19), kind=kLoop, calls=%fused_computation | loop fusion | flops 1492992 | bytes 1990656 | tf_op jit(solution)/shard_map/concatenate | solution.py:493
  4.6 104.1 %shard_map.113 = (bf16[224,384]{1,0:T(8,128)(2,1)}, bf16[224,384]{1,0:T(8,128)(2,1)}) custom-call(bf16[224,384]{1,0:T(8,128)(2,1)} %bitcast.24, bf16[224,384]{1,0:T(8,128)(2,1)} %bitcast.25, bf16[224,384]{1,0:T(8,128)(2,1)} %bitcast.26, f32[384]{0:T(512)} %gain_first_ref.1, f32[384]{0:T(512)} %gain_second_ref.1, f32[384]{0:T(512)} %bias_first_ref.1, ...), custom_call_target="tpu_custom_call" | custom-call | flops 5350883328 | bytes 1990656 | tf_op jit(solution)/shard_map/pallas_call | solution.py:498
  108.7 0.0 copy-start.1
  108.7 1.6 %copy.24 = bf16[2,1,112,384]{3,2,1,0:T(8,128)(2,1)} copy(bf16[2,1,112,384]{3,2,1,0:T(8,128)(2,1)} %bitcast.23) | data formatting | bytes 344064
  110.3 0.0 copy-done.1
  110.3 0.7 copy.25
Async XLA Ops:
  1.9 1.0 copy-start
  108.7 1.7 %copy-start.1 = (bf16[224,384]{1,0:T(8,128)(2,1)S(1)}, bf16[224,384]{1,0:T(8,128)(2,1)}, u32[]{:S(2)}) copy-start(bf16[224,384]{1,0:T(8,128)(2,1)} %get-tuple-element.5) | copy-start | bytes 516100
